TPU v7x, 512 devices: a whole 4x4x16 slice. The times are simulated.
512 devices in a mesh: view: 4 (over x_hi, core), brick: 128 (over z, y, x_lo).
Axes of the slice: x: 4 (x_hi: 2, x_lo: 2; x = x_hi * 2 + x_lo), y: 4, z: 16, core: 2. Of those that a mesh axis runs over, the one named last changes fastest.
Arguments:
- estimate: float32 [128, 2048, 128], P('brick'), may hold values from 0.5 to 2
- observed: float32 [4, 128, 2048, 128], P('view', None, 'brick'), may hold values from 0.25 to 4
- long_taps: float32 [4, 31], P('view'), may hold values from 0.05 to 1
- short_taps: float32 [4, 2, 7], P('view'), may hold values from 0.05 to 1
- brick_map: int32 [4, 128], P('view'), may hold values from 0 to 127, each once within a row
- valid_rows: int32 [4, 128], P('view'), may hold values from 512 to 2048
Outputs:
- refined: float32 [128, 2048, 128], P('brick')
Inputs may be any that keep to these rules, and one draw needn't show every extreme that they name: Each view's row of brick_map names every reference brick exactly once.
All inputs are finite; a program needn't handle non-finite values.
Results may differ from a plain program's by a relative error of at most 0.0001.
Values sent between devices are 32-bit elements; how exact they have to be, the bound alone decides.
A program may use at most 64 MiB of HBM per device.

v0:
```python
import jax
import jax.numpy as jnp
from jax import lax
from jax.sharding import PartitionSpec as P

ITERS = 2


def with_halo(block, sides, width):
    for axis, dim in sides:
        count = lax.axis_size(axis)
        forward = [(i, i + 1) for i in range(count - 1)]
        backward = [(target, source) for source, target in forward]
        low = lax.ppermute(
            lax.slice_in_dim(block, block.shape[dim] - width, None, axis=dim), axis, forward
        )
        high = lax.ppermute(lax.slice_in_dim(block, 0, width, axis=dim), axis, backward)
        block = jnp.concatenate([low, block, high], axis=dim)
    return block


def blur_axis(volume, kernel, dimension, adjoint):
    kernel_size = kernel.shape[0]
    radius = kernel_size // 2
    if adjoint:
        kernel = kernel[::-1]
    padding = [(0, 0)] * 3
    padding[dimension] = (radius, radius)
    padded = jnp.pad(volume, padding)
    length = volume.shape[dimension]
    summed = jnp.zeros(volume.shape, jnp.float32)
    for offset in range(kernel_size):
        summed = summed + kernel[offset] * lax.slice_in_dim(
            padded, offset, offset + length, axis=dimension
        )
    return summed


def blur_rows(volume, kernel, adjoint):
    kernel_size = kernel.shape[0]
    radius = kernel_size // 2
    if adjoint:
        kernel = kernel[::-1]
    padded = with_halo(volume, (("brick", 1),), radius)
    length = volume.shape[1]
    summed = jnp.zeros(volume.shape, jnp.float32)
    for offset in range(kernel_size):
        summed = summed + kernel[offset] * lax.slice_in_dim(padded, offset, offset + length, axis=1)
    return summed


def to_view(volume, forward_map):
    arrived = lax.all_to_all(volume, "brick", split_axis=1, concat_axis=0, tiled=True)
    brick_count = forward_map.shape[0]
    bricks = arrived.reshape(brick_count, -1, arrived.shape[1], arrived.shape[2])
    return bricks[forward_map].reshape(arrived.shape)


def to_reference(volume, inverse):
    brick_count = inverse.shape[0]
    bricks = volume.reshape(brick_count, -1, volume.shape[1], volume.shape[2])
    ordered = bricks[inverse].reshape(volume.shape)
    return lax.all_to_all(ordered, "brick", split_axis=0, concat_axis=1, tiled=True)


def on_device(estimate, observed, long_taps, short_taps, brick_map, valid_rows):
    kernel_long = long_taps[0] / jnp.sum(long_taps[0])
    kernel_plane = short_taps[0, 0] / jnp.sum(short_taps[0, 0])
    kernel_column = short_taps[0, 1] / jnp.sum(short_taps[0, 1])
    forward_map = brick_map[0]
    inverse = jnp.argsort(forward_map)
    observed_view = observed[0]
    row_count = observed_view.shape[1]
    row_ids = lax.axis_index("brick") * row_count + jnp.arange(row_count, dtype=jnp.int32)
    limits = jnp.repeat(valid_rows[0], observed_view.shape[0] // forward_map.shape[0])
    valid_mask = (row_ids[None, :] < limits[:, None])[:, :, None]
    current = estimate
    for iteration in range(ITERS):
        framed = to_view(current, forward_map)
        blurred = blur_rows(framed, kernel_long, False)
        blurred = blur_axis(blur_axis(blurred, kernel_plane, 0, False), kernel_column, 2, False)
        ratios = jnp.where(valid_mask, observed_view / blurred, 1.0)
        spread_back = blur_axis(blur_axis(ratios, kernel_plane, 0, True), kernel_column, 2, True)
        correction = to_reference(blur_rows(spread_back, kernel_long, True), inverse)
        log_terms = jnp.log(correction)
        current = current * jnp.exp(lax.psum(log_terms, "view"))
    return current


def solution(mesh):
    placed = (
        P("brick", None, None),
        P("view", None, "brick", None),
        P("view", None),
        P("view", None, None),
        P("view", None),
        P("view", None),
    )
    return jax.shard_map(
        on_device, mesh=mesh, in_specs=placed, out_specs=P("brick", None, None), check_vma=False
    )
```

profile of v0, /device:TPU:1, one launch (start us, length us, event | category | flops | bytes accessed | tf_op | source)
XLA Modules:
  0.0 746.9 jit_solution(6758244654196915608)
XLA Ops:
  6.5 21.6 %all-to-all-start = ((f32[1,2048,128]{2,0,1:T(1,128)}), f32[1,2048,128]{2,0,1:T(1,128)S(1)}, u32[]{:S(2)}, u32[]{:S(2)}) async-start(f32[1,2048,128]{2,0,1:T(1,128)} %bitcast.120), calls=%async_computation | async-start | bytes 2097152 | tf_op jit(solution)/shard_map/all_to_all | solution.py:53
  29.7 1.3 broadcast_divide_fusion.2
  33.7 43.9 %all-to-all-done = f32[1,2048,128]{2,0,1:T(1,128)S(1)} async-done(((f32[1,2048,128]{2,0,1:T(1,128)}), f32[1,2048,128]{2,0,1:T(1,128)S(1)}, u32[]{:S(2)}, u32[]{:S(2)}) %all-to-all-start) | async-done | bytes 1048608 | tf_op jit(solution)/shard_map/all_to_all | solution.py:53
  77.5 0.8 gather_fusion
  79.1 3.0 collective-permute-start
  82.1 1.3 collective-permute-start.1
  86.4 33.4 %collective-permute-done = f32[128,15,128]{2,0,1:T(8,128)S(1)} collective-permute-done((f32[128,15,128]{2,0,1:T(8,128)S(1)}, f32[128,15,128]{2,0,1:T(8,128)S(1)}, u32[]{:S(2)}, u32[]{:S(2)}) %collective-permute-start) | collective-permute-done | bytes 983072 | tf_op jit(solution)/shard_map/ppermute | solution.py:14
  121.0 24.0 %fusion.299 = f32[128,16,128]{2,1,0:T(8,128)S(1)} fusion(f32[128,15,128]{2,1,0:T(8,128)S(1)} %copy.13, f32[128,16,128]{2,1,0:T(8,128)S(1)} %gather_fusion, f32[128,31,128]{2,1,0:T(8,128)S(1)} %copy_dynamic-update-slice_fusion.1, f32[]{:T(128)} %bitcast.44, f32[]{:T(128)} %bitcast.43, f32[]{:T(128)} %bitcast.42, f32[]{:T(128)} %bitcast.41, f32[]{:T(128)} %bitcast.40, ...), kind=kLoop, calls=%fused_computation.495 | loop fusion | flops 19922944 | bytes 18808956 | tf_op jit(solution)/shard_map/add | solution.py:48
  145.0 4.9 multiply_add_fusion.3
  149.9 6.3 fusion.357
  156.2 4.9 multiply_add_fusion.2
  161.1 6.1 fusion.19
  167.4 1.2 copy.18
  168.6 1.3 collective-permute-start.3
  169.9 1.3 copy.16
  171.2 5.9 collective-permute-start.2
  177.2 2.6 sort.17
  181.2 9.6 %collective-permute-done.3 = f32[128,15,128]{2,0,1:T(8,128)} collective-permute-done((f32[128,15,128]{2,0,1:T(8,128)}, f32[128,15,128]{2,0,1:T(8,128)}, u32[]{:S(2)}, u32[]{:S(2)}) %collective-permute-start.3) | collective-permute-done | bytes 983072 | tf_op jit(solution)/shard_map/ppermute | solution.py:17
  190.8 1.8 copy.19
  192.6 26.0 %collective-permute-done.2 = f32[128,15,128]{2,0,1:T(8,128)S(1)} collective-permute-done((f32[128,15,128]{2,0,1:T(8,128)}, f32[128,15,128]{2,0,1:T(8,128)S(1)}, u32[]{:S(2)}, u32[]{:S(2)}) %collective-permute-start.2) | collective-permute-done | bytes 983072 | tf_op jit(solution)/shard_map/ppermute | solution.py:14
  219.1 25.1 %fusion.197 = f32[128,16,128]{2,1,0:T(8,128)S(1)} fusion(f32[128,16,128]{2,1,0:T(8,128)S(1)} %fusion.19, f32[128,15,128]{2,1,0:T(8,128)S(1)} %copy.19, f32[128,15,128]{2,1,0:T(8,128)S(1)} %copy.17, f32[]{:T(128)} %bitcast.98, f32[]{:T(128)} %bitcast.97, f32[]{:T(128)} %bitcast.96, f32[]{:T(128)} %bitcast.95, f32[]{:T(128)} %bitcast.94, f32[]{:T(128)} %bitcast.93, ...), kind=kLoop, calls=%fused_computation.393 | loop fusion | flops 23855104 | bytes 4063356 | tf_op jit(solution)/shard_map/add | solution.py:48
  244.3 0.8 gather_fusion.1
  245.1 67.0 %all_to_all.16 = f32[128,16,128]{2,1,0:T(8,128)S(1)} all-to-all(f32[128,16,128]{2,1,0:T(8,128)S(1)} %gather_fusion.1), channel_id=1, replica_groups=mesh['view'=4,'brick'=128] {'brick'}, dimensions={0} | all-to-all | bytes 2097152 | tf_op jit(solution)/shard_map/all_to_all | solution.py:63
  312.0 1.1 log.28
  313.2 58.4 %all-reduce.11.cloned.1.call-done = f32[1,2048,128]{2,1,0:T(8,128)} async-done(((f32[1,2048,128]{2,1,0:T(8,128)}), f32[1,2048,128]{2,1,0:T(8,128)}) %all-reduce.11.cloned.1.call-update) | async-done | bytes 1048592 | tf_op jit(solution)/shard_map/psum | solution.py:86
  371.6 1.4 exponential_multiply_fusion.1
  373.0 66.2 %all_to_all.17 = f32[1,2048,128]{2,0,1:T(1,128)S(1)} all-to-all(f32[1,2048,128]{2,0,1:T(1,128)S(1)} %bitcast.119), channel_id=1, replica_groups=mesh['view'=4,'brick'=128] {'brick'}, dimensions={1} | all-to-all | bytes 2097152 | tf_op jit(solution)/shard_map/all_to_all | solution.py:53
  439.2 0.8 gather_fusion.2
  440.5 2.5 collective-permute-start.4
  443.3 1.5 collective-permute-start.5
  445.0 35.9 %collective-permute-done.4 = f32[128,15,128]{2,0,1:T(8,128)S(1)} collective-permute-done((f32[128,15,128]{2,0,1:T(8,128)S(1)}, f32[128,15,128]{2,0,1:T(8,128)S(1)}, u32[]{:S(2)}, u32[]{:S(2)}) %collective-permute-start.4) | collective-permute-done | bytes 983072 | tf_op jit(solution)/shard_map/ppermute | solution.py:14
  481.5 0.8 collective-permute-done.5
  482.8 24.0 %fusion.155 = f32[128,16,128]{2,1,0:T(8,128)S(1)} fusion(f32[128,15,128]{2,1,0:T(8,128)S(1)} %copy.22, f32[128,16,128]{2,1,0:T(8,128)S(1)} %gather_fusion.2, f32[128,31,128]{2,1,0:T(8,128)S(1)} %copy_dynamic-update-slice_fusion, f32[]{:T(128)} %bitcast.44, f32[]{:T(128)} %bitcast.43, f32[]{:T(128)} %bitcast.42, f32[]{:T(128)} %bitcast.41, f32[]{:T(128)} %bitcast.40, ...), kind=kLoop, calls=%fused_computation.351 | loop fusion | flops 19922944 | bytes 18808956 | tf_op jit(solution)/shard_map/add | solution.py:48
  506.8 4.9 multiply_add_fusion.1
  511.7 6.3 fusion.356
  518.1 4.9 multiply_add_fusion
  522.9 6.1 fusion.44
  529.6 1.3 collective-permute-start.7
  531.2 8.0 %collective-permute-start.6 = (f32[128,15,128]{2,0,1:T(8,128)S(1)}, f32[128,15,128]{2,0,1:T(8,128)S(1)}, u32[]{:S(2)}, u32[]{:S(2)}) collective-permute-start(f32[128,15,128]{2,0,1:T(8,128)S(1)} %copy.25), channel_id=1, source_target_pairs={{0,1},{1,2},{2,3},{3,4},{4,5},{5,6},{6,7},{7,8},{8,9},{9,10},{10,1... | collective-permute-start | bytes 2949128 | tf_op jit(solution)/shard_map/ppermute | solution.py:14
  539.2 16.0 %collective-permute-done.7 = f32[128,15,128]{2,0,1:T(8,128)S(1)} collective-permute-done((f32[128,15,128]{2,0,1:T(8,128)S(1)}, f32[128,15,128]{2,0,1:T(8,128)S(1)}, u32[]{:S(2)}, u32[]{:S(2)}) %collective-permute-start.7) | collective-permute-done | bytes 983072 | tf_op jit(solution)/shard_map/ppermute | solution.py:17
  555.8 24.8 %collective-permute-done.6 = f32[128,15,128]{2,0,1:T(8,128)S(1)} collective-permute-done((f32[128,15,128]{2,0,1:T(8,128)S(1)}, f32[128,15,128]{2,0,1:T(8,128)S(1)}, u32[]{:S(2)}, u32[]{:S(2)}) %collective-permute-start.6) | collective-permute-done | bytes 983072 | tf_op jit(solution)/shard_map/ppermute | solution.py:14
  580.7 1.5 copy.26
  582.2 31.2 %fusion.53 = f32[128,16,128]{2,1,0:T(8,128)S(1)} fusion(f32[128,16,128]{2,1,0:T(8,128)S(1)} %fusion.44, f32[128,15,128]{2,1,0:T(8,128)S(1)} %copy.28, f32[128,15,128]{2,1,0:T(8,128)} %copy.26, f32[]{:T(128)} %bitcast.98, f32[]{:T(128)} %bitcast.97, f32[]{:T(128)} %bitcast.96, f32[]{:T(128)} %bitcast.95, f32[]{:T(128)} %bitcast.94, f32[]{:T(128)} %bitcast.93, ...), kind=kLoop, calls=%fused_computation.249 | loop fusion | flops 23855104 | bytes 4063356 | tf_op jit(solution)/shard_map/add | solution.py:48
  613.4 0.8 gather_fusion.3
  614.2 64.9 %all_to_all.18 = f32[128,16,128]{2,1,0:T(8,128)S(1)} all-to-all(f32[128,16,128]{2,1,0:T(8,128)S(1)} %gather_fusion.3), channel_id=1, replica_groups=mesh['view'=4,'brick'=128] {'brick'}, dimensions={0} | all-to-all | bytes 2097152 | tf_op jit(solution)/shard_map/all_to_all | solution.py:63
  679.0 1.1 log.30
  680.2 57.6 %all-reduce.13.cloned.1.call-done = f32[1,2048,128]{2,1,0:T(8,128)} async-done(((f32[1,2048,128]{2,1,0:T(8,128)}), f32[1,2048,128]{2,1,0:T(8,128)}) %all-reduce.13.cloned.1.call-update) | async-done | bytes 1048592 | tf_op jit(solution)/shard_map/psum | solution.py:86
  737.7 2.3 exponential_multiply_fusion
  (59 shorter events, 14.9 us)
Async XLA Ops:
  6.5 21.6 %copy-start.4 = (f32[1,31]{1,0:T(1,128)S(1)}, f32[1,31]{1,0:T(1,128)}, u32[]{:S(2)}) copy-start(f32[1,31]{1,0:T(1,128)} %param.8) | copy-start | bytes 376
  6.5 22.3 %copy-start.3 = (f32[1,2,7]{2,1,0:T(2,128)S(1)}, f32[1,2,7]{2,1,0:T(2,128)}, u32[]{:S(2)}) copy-start(f32[1,2,7]{2,1,0:T(2,128)} %param.9) | copy-start | bytes 172
  6.5 23.2 %copy-start.6 = (s32[1,128]{1,0:T(1,128)S(1)}, s32[1,128]{1,0:T(1,128)}, u32[]{:S(2)}) copy-start(s32[1,128]{1,0:T(1,128)} %param.10) | copy-start | bytes 1540
  6.5 71.0 %all-to-all-start = ((f32[1,2048,128]{2,0,1:T(1,128)}), f32[1,2048,128]{2,0,1:T(1,128)S(1)}, u32[]{:S(2)}, u32[]{:S(2)}) async-start(f32[1,2048,128]{2,0,1:T(1,128)} %bitcast.120), calls=%async_computation | async-start | bytes 2097152 | tf_op jit(solution)/shard_map/all_to_all | solution.py:53
  28.1 343.5 %all-reduce.11.cloned.1.call-start = ((), (), s32[]{:S(2)}) async-start(), calls=%async_computation.4 | async-start | bytes 2097152 | tf_op jit(solution)/shard_map/psum | solution.py:86
  78.4 7.8 %copy-start.5 = (s32[1,128]{1,0:T(1,128)S(1)}, s32[1,128]{1,0:T(1,128)}, u32[]{:S(2)}) copy-start(s32[1,128]{1,0:T(1,128)} %param.11) | copy-start | bytes 1540
  79.1 40.7 %collective-permute-start = (f32[128,15,128]{2,0,1:T(8,128)S(1)}, f32[128,15,128]{2,0,1:T(8,128)S(1)}, u32[]{:S(2)}, u32[]{:S(2)}) collective-permute-start(f32[128,15,128]{2,0,1:T(8,128)S(1)} %copy.12), channel_id=1, source_target_pairs={{0,1},{1,2},{2,3},{3,4},{4,5},{5,6},{6,7},{7,8},{8,9},{9,10},{10,1... | collective-permute-start | bytes 2949128 | tf_op jit(solution)/shard_map/ppermute | solution.py:14
  82.1 38.3 %collective-permute-start.1 = (f32[128,15,128]{2,0,1:T(8,128)S(1)}, f32[128,15,128]{2,0,1:T(8,128)S(1)}, u32[]{:S(2)}, u32[]{:S(2)}) collective-permute-start(f32[128,15,128]{2,0,1:T(8,128)S(1)} %copy.14), channel_id=1, source_target_pairs={{1,0},{2,1},{3,2},{4,3},{5,4},{6,5},{7,6},{8,7},{9,8},{10,9},{11,1... | collective-permute-start | bytes 2949128 | tf_op jit(solution)/shard_map/ppermute | solution.py:17
  145.0 4.9 copy-start.1
  168.6 22.1 %collective-permute-start.3 = (f32[128,15,128]{2,0,1:T(8,128)}, f32[128,15,128]{2,0,1:T(8,128)}, u32[]{:S(2)}, u32[]{:S(2)}) collective-permute-start(f32[128,15,128]{2,0,1:T(8,128)} %copy.18), channel_id=1, source_target_pairs={{1,0},{2,1},{3,2},{4,3},{5,4},{6,5},{7,6},{8,7},{9,8},{10,9},{11,1... | collective-permute-start | bytes 2949128 | tf_op jit(solution)/shard_map/ppermute | solution.py:17
  171.2 47.3 %collective-permute-start.2 = (f32[128,15,128]{2,0,1:T(8,128)}, f32[128,15,128]{2,0,1:T(8,128)S(1)}, u32[]{:S(2)}, u32[]{:S(2)}) collective-permute-start(f32[128,15,128]{2,0,1:T(8,128)} %copy.16), channel_id=1, source_target_pairs={{0,1},{1,2},{2,3},{3,4},{4,5},{5,6},{6,7},{7,8},{8,9},{9,10},{10,1... | collective-permute-start | bytes 2949128 | tf_op jit(solution)/shard_map/ppermute | solution.py:14
  312.0 59.6 %copy-start = (f32[1,2048,128]{2,1,0:T(8,128)S(1)}, f32[1,2048,128]{2,1,0:T(8,128)}, u32[]{:S(2)}) copy-start(f32[1,2048,128]{2,1,0:T(8,128)} %param.6) | copy-start | bytes 3145732
  313.2 424.6 %all-reduce.13.cloned.1.call-start = ((), (), s32[]{:S(2)}) async-start(), calls=%async_computation.5 | async-start | bytes 2097152 | tf_op jit(solution)/shard_map/psum | solution.py:86
  440.5 40.4 %collective-permute-start.4 = (f32[128,15,128]{2,0,1:T(8,128)S(1)}, f32[128,15,128]{2,0,1:T(8,128)S(1)}, u32[]{:S(2)}, u32[]{:S(2)}) collective-permute-start(f32[128,15,128]{2,0,1:T(8,128)S(1)} %copy.21), channel_id=1, source_target_pairs={{0,1},{1,2},{2,3},{3,4},{4,5},{5,6},{6,7},{7,8},{8,9},{9,10},{10,1... | collective-permute-start | bytes 2949128 | tf_op jit(solution)/shard_map/ppermute | solution.py:14
  443.3 38.9 %collective-permute-start.5 = (f32[128,15,128]{2,0,1:T(8,128)S(1)}, f32[128,15,128]{2,0,1:T(8,128)S(1)}, u32[]{:S(2)}, u32[]{:S(2)}) collective-permute-start(f32[128,15,128]{2,0,1:T(8,128)S(1)} %copy.23), channel_id=1, source_target_pairs={{1,0},{2,1},{3,2},{4,3},{5,4},{6,5},{7,6},{8,7},{9,8},{10,9},{11,1... | collective-permute-start | bytes 2949128 | tf_op jit(solution)/shard_map/ppermute | solution.py:17
  506.8 4.9 copy-start.2
  529.6 25.7 %collective-permute-start.7 = (f32[128,15,128]{2,0,1:T(8,128)S(1)}, f32[128,15,128]{2,0,1:T(8,128)S(1)}, u32[]{:S(2)}, u32[]{:S(2)}) collective-permute-start(f32[128,15,128]{2,0,1:T(8,128)S(1)} %copy.27), channel_id=1, source_target_pairs={{1,0},{2,1},{3,2},{4,3},{5,4},{6,5},{7,6},{8,7},{9,8},{10,9},{11,1... | collective-permute-start | bytes 2949128 | tf_op jit(solution)/shard_map/ppermute | solution.py:17
  531.2 49.5 %collective-permute-start.6 = (f32[128,15,128]{2,0,1:T(8,128)S(1)}, f32[128,15,128]{2,0,1:T(8,128)S(1)}, u32[]{:S(2)}, u32[]{:S(2)}) collective-permute-start(f32[128,15,128]{2,0,1:T(8,128)S(1)} %copy.25), channel_id=1, source_target_pairs={{0,1},{1,2},{2,3},{3,4},{4,5},{5,6},{6,7},{7,8},{8,9},{9,10},{10,1... | collective-permute-start | bytes 2949128 | tf_op jit(solution)/shard_map/ppermute | solution.py:14
Sparse Core Ops, SparseCore 0:
  313.3 58.3 all-reduce.10
  680.3 57.4 all-reduce.12
where the time goes:
time: 749 us; the launch traced here: 747 us
  waiting for transfers between devices  306 us (41%)
  blocking collectives  198 us (26%)
  other arithmetic  159 us (21%)
  starting transfers between devices  46.5 us (6%)
  local copies, waits for them, and re-layouts  23.3 us (3%)
  between operations  13.8 us (2%)
    all_to_all x2, blocking collectives, to_reference(): lax.all_to_all(ordered, 'brick', split_axis=0, concat_axis=1, tiled=True)  132 us
    ppermute x4, waiting for transfers between devices, with_halo(): lax.ppermute(lax.slice_in_dim(block, block.shape[dim] - width, None, axis...  120 us
    psum x2, waiting for transfers between devices, on_device(): current = current * jnp.exp(lax.psum(log_terms, 'view'))  116 us
    add x4, other arithmetic, blur_rows(): summed + kernel[offset] * lax.slice_in_dim(padded, offset, offset + lengt...  104 us
    all_to_all x1, blocking collectives, to_view(): lax.all_to_all(volume, 'brick', split_axis=1, concat_axis=0, tiled=True)  66.2 us
    all_to_all x1, waiting for transfers between devices, to_view(): lax.all_to_all(volume, 'brick', split_axis=1, concat_axis=0, tiled=True)  43.9 us
    add x6, other arithmetic, blur_axis(): summed + kernel[offset] * lax.slice_in_dim(padded, offset, offset + lengt...  31.8 us
    ppermute x4, waiting for transfers between devices, with_halo(): lax.ppermute(lax.slice_in_dim(block, 0, width, axis=dim), axis, backward)  26.4 us
  transfers between devices with their start and end apart: 11, of which 10 were waited for; matrix products, arithmetic and copies ran while one was open for 2% of the time, Pallas kernels for 0%

commit v1 on v0

v1 whole, which is shorter than its diff:
```python
import jax
import jax.numpy as jnp
from jax import lax
from jax.experimental import pallas as pl
from jax.experimental.pallas import tpu as pltpu
from jax.sharding import Mesh
from jax.sharding import PartitionSpec as P

F32, BF16 = jnp.float32, jnp.bfloat16
ITERS = 2
VIEWS, BRICKS, ROWS, COLS = 4, 128, 2048, 128
NZ, NY = 16, 4
BLOCK = 128
OWN = 4
WIDE = OWN + 6
HALO = 16
TALL = BLOCK + 2 * HALO
AXES = ("xh", "core", "z", "y", "xl")
MESH = pl.DeviceIdType.MESH


def split(x):
    head = x.astype(BF16)
    return head, (x - head.astype(F32)).astype(BF16)


def dot3(ah, al, bh, bl):
    def dot(a, b):
        return jnp.dot(a, b, preferred_element_type=F32)

    return dot(ah, bh) + (dot(al, bh) + dot(ah, bl))


def exchange_halves(a, b):
    axis = a.ndim - 2
    top = lax.broadcasted_iota(jnp.int32, a.shape, axis) < 4
    first = jnp.where(top, a, pltpu.roll(b, 4, axis))
    second = jnp.where(top, pltpu.roll(a, 4, axis), b)
    return first, second


def loop(n, body):
    def step(i, carry):
        body(i)
        return carry

    lax.fori_loop(0, n, step, 0)


def kernel(
    est, obs, long_taps, short_taps, brick_map, valid_rows, out,
    par, turned, s1, r1, s2, r2, obs_out, obs_in, ext, rows_done, spread, tall, corr,
    x2, r3, s4, gathered, tile_taps, bf_h, bf_l, bb_h, bb_l, tf_h, tf_l, tb_h, tb_l,
    par_s, par_r, z_s, z_r, obs_s, obs_r, p_s, p_r, ec_s, ec_r, er_s, er_r, uc_s, uc_r, ur_s, ur_r,
    q_s, q_r, y_s, y_r, v_s, v_r,
):
    xh, core, z, y, xl = (lax.axis_index(a) for a in AXES)
    x = 2 * xh + xl
    kk = 4 * xl + lax.rem(y + x, NY)
    k = 8 * xh + kk
    g = 2 * k + core
    view = 2 * xh + core
    slab = 2 * y + xl
    place = view * 8 + slab

    def at_kk(xh_, core_, kk_):
        xl_ = kk_ // 4
        return xh_, core_, z, lax.rem(lax.rem(kk_, 4) + 8 - 2 * xh_ - xl_, NY), xl_

    def slab_of(kk_):
        _, _, _, y_, xl_ = at_kk(xh, core, kk_)
        return 2 * y_ + xl_

    def at_g(g_):
        k_ = g_ // 2
        return at_kk(k_ // 8, lax.rem(g_, 2), lax.rem(k_, 8))

    def at_z(z_):
        return xh, core, z_, y, xl

    def at_place(place_):
        return place_ // 16, lax.rem(place_ // 8, 2), z, lax.rem(place_ // 2, 4), lax.rem(place_, 2)

    def at_view(view_):
        return view_ // 2, lax.rem(view_, 2), z, y, xl

    def g_of(place_):
        xh_, _, _, y_, xl_ = at_place(place_)
        x_ = 2 * xh_ + xl_
        return 2 * (4 * x_ + lax.rem(y_ + x_, NY)) + lax.rem(place_ // 8, 2)

    def remote(src, dst, send, recv, device):
        return pltpu.make_async_remote_copy(
            src_ref=src, dst_ref=dst, send_sem=send, recv_sem=recv, device_id=device, device_id_type=MESH
        )

    left, right = lax.rem(g + 31, 32), lax.rem(g + 1, 32)
    above, below = lax.rem(z + NZ - 1, NZ), lax.rem(z + 1, NZ)

    barrier = pltpu.get_barrier_semaphore()

    @pl.loop(1, NZ)
    def _(d):
        pl.semaphore_signal(barrier, inc=1, device_id=at_z(lax.rem(z + d, NZ)), device_id_type=MESH)

    @pl.loop(1, 32)
    def _(n):
        pl.semaphore_signal(barrier, inc=1, device_id=at_place(lax.rem(place + n, 32)), device_id_type=MESH)

    par[view] = jnp.zeros((8, 128), F32)
    par[view, 0:1, :] = brick_map[...].astype(F32)
    par[view, 1:2, :] = valid_rows[...].astype(F32)
    par[view, 2:3, 0:31] = long_taps[...]
    par[view, 3:5, 0:7] = short_taps[...]

    pl.semaphore_wait(barrier, NZ - 1 + 31)

    def par_copy(m, source, device):
        return remote(par.at[source], par.at[source], par_s.at[m], par_r.at[m], device)

    for m in range(1, VIEWS):
        par_copy(m, view, at_view(lax.rem(view + m, VIEWS))).start()

    def piece_for(zt):
        block = est[pl.ds(pl.multiple_of(BLOCK * zt, BLOCK), BLOCK), :]
        turned[...] = block.T
        half = turned[pl.ds(pl.multiple_of(64 * xh, 64), 64), :].reshape(4, 2, 8, 128)
        first, second = exchange_halves(half[:, 0], half[:, 1])
        return jnp.where(core == 0, first, second)

    def z_copy(d, source, device):
        return remote(s1.at[d], r1.at[source], z_s.at[d], z_r.at[d], device)

    def far_first(i):
        return 8 + ((i + 1) // 2) * (1 - 2 * lax.rem(i, 2))

    @pl.loop(0, NZ - 1)
    def _(i):
        d = far_first(i)
        zt = lax.rem(z + d, NZ)
        s1[d] = piece_for(zt)
        z_copy(d, z, at_z(zt)).start()

    r1[z] = piece_for(z)

    @pl.loop(0, 16)
    def _(r):
        obs_out[pl.ds(r, 128, stride=16), :] = obs[pl.ds(r, 128, stride=16), :].T

    def obs_copy(n, g_, view_, slab_, device):
        src = obs_out.at[pl.ds(pl.multiple_of(64 * g_, 64), 64)]
        return remote(src, obs_in.at[view_, slab_], obs_s.at[n], obs_r.at[n], device)

    @pl.loop(1, 32)
    def _(n):
        to = lax.rem(place + n, 32)
        obs_copy(n, g_of(to), view, slab, at_place(to)).start()

    obs_in[view, slab] = obs_out[pl.ds(pl.multiple_of(64 * g, 64), 64), :]

    for m in range(1, VIEWS):
        par_copy(m, lax.rem(view + VIEWS - m, VIEWS), at_view(lax.rem(view + m, VIEWS))).wait_recv()
    lane = lax.broadcasted_iota(jnp.int32, (1, 128), 1)
    order = lax.broadcasted_iota(jnp.int32, (128, 128), 0)
    brick = (lax.rem(order, 16) * 8 + order // 16).astype(F32)
    tall_lane = lax.broadcasted_iota(jnp.int32, (BLOCK, TALL), 1)
    inside = jnp.logical_and(
        jnp.logical_or(tall_lane >= HALO, z > 0), jnp.logical_or(tall_lane < HALO + BLOCK, z < NZ - 1)
    )
    for v in range(VIEWS):
        bricks, long_row, plane, column = (par[v, i : i + 1, :] for i in (0, 2, 3, 4))
        long_row, plane, column = (t / jnp.sum(t, axis=1, keepdims=True) for t in (long_row, plane, column))
        matrix = jnp.zeros((128, 128), F32)
        for t in range(7):
            near = pltpu.roll(bricks, (3 - t) % 128, 1)
            near = jnp.where(jnp.logical_and(lane + (t - 3) >= 0, lane + (t - 3) < BRICKS), near, -1.0)
            matrix += jnp.where(brick == near, plane[:, t : t + 1], 0.0)
            tile_taps[8 * v + t : 8 * v + t + 1, :] = jnp.broadcast_to(column[:, t : t + 1], (1, 128))
        bf_h[v], bf_l[v] = split(matrix)
        bb_h[v], bb_l[v] = split(matrix.T)
        padded = jnp.concatenate([long_row, jnp.zeros((1, 128), F32)], axis=1)
        wide = jnp.broadcast_to(padded, (BLOCK, 256))
        toeplitz = pltpu.roll(wide, 1, 1, stride=1, stride_axis=0)[:, :TALL]
        tf_h[pl.ds(BLOCK * v, BLOCK), :], tf_l[pl.ds(BLOCK * v, BLOCK), :] = split(
            jnp.where(inside, toeplitz, 0.0)
        )
        high = jnp.broadcast_to(padded, (256, 256))
        flipped = pltpu.roll(high, 225, 1, stride=1, stride_axis=0)[:, :128].T[:, :TALL]
        tb_h[pl.ds(BLOCK * v, BLOCK), :], tb_l[pl.ds(BLOCK * v, BLOCK), :] = split(
            jnp.where(inside, flipped, 0.0)
        )

    @pl.loop(0, NZ - 1)
    def _(i):
        d = far_first(i)
        z_copy(d, lax.rem(z + NZ - d, NZ), at_z(lax.rem(z + d, NZ))).wait_recv()

    @pl.loop(0, 8)
    def _(m):
        first, second = exchange_halves(r1[2 * m], r1[2 * m + 1])
        for i in range(4):
            s2[pl.ds(pl.multiple_of(64 * (2 * i) + 8 * m, 8), 8), :] = first[i]
            s2[pl.ds(pl.multiple_of(64 * (2 * i + 1) + 8 * m, 8), 8), :] = second[i]

    def p_copy(n, kt, source):
        src = s2.at[pl.ds(pl.multiple_of(64 * kt, 64), 64)]
        dst = r2.at[pl.ds(pl.multiple_of(64 * slab_of(source), 64), 64)]
        return remote(src, dst, p_s.at[n], p_r.at[n], at_kk(xh, core, kt))

    @pl.loop(1, 8)
    def _(n):
        p_copy(n, lax.rem(kk + n, 8), kk).start()

    mine = pl.ds(pl.multiple_of(64 * slab, 64), 64)
    r2[mine, :] = s2[pl.ds(pl.multiple_of(64 * kk, 64), 64), :]

    @pl.loop(1, 8)
    def _(n):
        p_copy(n, lax.rem(kk + n, 8), lax.rem(kk + 8 - n, 8)).wait_recv()

    for c in range(OWN):
        ext[0, 3 + c, HALO : HALO + BLOCK, :] = r2[pl.ds(c, 128, stride=4), :].T

    @pl.loop(1, 32)
    def _(n):
        source = lax.rem(place + 32 - n, 32)
        to = lax.rem(place + n, 32)
        obs_copy(n, g_of(to), source // 8, lax.rem(source, 8), at_place(to)).wait_recv()

    middle = pl.ds(HALO, BLOCK)

    def ext_columns(it):
        return (
            remote(ext.at[it, 3:6, middle], ext.at[it, 7:10, middle], ec_s.at[it, 0], ec_r.at[it, 0], at_g(left)),
            remote(ext.at[it, 4:7, middle], ext.at[it, 0:3, middle], ec_s.at[it, 1], ec_r.at[it, 1], at_g(right)),
        )

    def ext_rows(it):
        first, last = pl.ds(HALO, HALO), pl.ds(BLOCK, HALO)
        return (
            remote(ext.at[it, :, first], ext.at[it, :, pl.ds(HALO + BLOCK, HALO)], er_s.at[it, 0], er_r.at[it, 0], at_z(above)),
            remote(ext.at[it, :, last], ext.at[it, :, pl.ds(0, HALO)], er_s.at[it, 1], er_r.at[it, 1], at_z(below)),
        )

    def spread_columns(it, v):
        return (
            remote(spread.at[it, v, 3:6], spread.at[it, v, 7:10], uc_s.at[it, v, 0], uc_r.at[it, v, 0], at_g(left)),
            remote(spread.at[it, v, 4:7], spread.at[it, v, 0:3], uc_s.at[it, v, 1], uc_r.at[it, v, 1], at_g(right)),
        )

    def tall_rows(it, v):
        first, last = pl.ds(HALO, HALO), pl.ds(BLOCK, HALO)
        return (
            remote(tall.at[it, v, :, first], tall.at[it, v, :, pl.ds(HALO + BLOCK, HALO)], ur_s.at[it, v, 0], ur_r.at[it, v, 0], at_z(above)),
            remote(tall.at[it, v, :, last], tall.at[it, v, :, pl.ds(0, HALO)], ur_s.at[it, v, 1], ur_r.at[it, v, 1], at_z(below)),
        )

    def column_inside(i):
        at = OWN * g + i - 3
        return jnp.logical_and(at >= 0, at < COLS)

    row_ids = (BLOCK * z + lax.broadcasted_iota(jnp.int32, (BLOCK, 128), 0)).astype(F32)

    for it in range(ITERS):
        for copy in ext_columns(it):
            copy.start()
        for copy in ext_columns(it):
            copy.wait_recv()
        for copy in ext_rows(it):
            copy.start()
        for copy in ext_rows(it):
            copy.wait_recv()

        @pl.loop(0, WIDE)
        def _(i):
            head, tail = split(jnp.where(column_inside(i), ext[it, i], 0.0))
            rows_done[i] = dot3(tf_h[...], tf_l[...], head, tail)

        @pl.loop(0, VIEWS)
        def _(v):
            part = pl.ds(pl.multiple_of(BLOCK * v, BLOCK), BLOCK)

            @pl.loop(0, OWN)
            def _(c):
                blurred = jnp.zeros((BLOCK, 128), F32)
                for t in range(7):
                    blurred += tile_taps[pl.ds(8 * v + t, 1), :] * rows_done[c + t, part, :]
                blurred = dot3(*split(blurred), bf_h[v], bf_l[v])
                seen = obs_in[v, :, pl.ds(pl.multiple_of(16 * c, 16), 16), :].reshape(BLOCK, 128)
                ratio = jnp.where(row_ids < par[v, 1:2, :], seen / blurred, 1.0)
                spread[it, v, 3 + c] = dot3(*split(ratio), bb_h[v], bb_l[v])

            for copy in spread_columns(it, v):
                copy.start()

        @pl.loop(0, VIEWS)
        def _(v):
            for copy in spread_columns(it, v):
                copy.wait_recv()

            @pl.loop(0, OWN)
            def _(c):
                total = jnp.zeros((BLOCK, 128), F32)
                for t in range(7):
                    tap = jnp.where(column_inside(c + t), tile_taps[pl.ds(8 * v + 6 - t, 1), :], 0.0)
                    total += tap * spread[it, v, c + t]
                tall[it, v, c, HALO : HALO + BLOCK, :] = total

            for copy in tall_rows(it, v):
                copy.start()

        @pl.loop(0, VIEWS)
        def _(v):
            for copy in tall_rows(it, v):
                copy.wait_recv()
            part = pl.ds(pl.multiple_of(BLOCK * v, BLOCK), BLOCK)

            @pl.loop(0, OWN)
            def _(c):
                corr[v, c] = dot3(tb_h[part, :], tb_l[part, :], *split(tall[it, v, c]))

        for c in range(OWN):
            log_total = jnp.log(corr[0, c] * corr[1, c]) + jnp.log(corr[2, c] * corr[3, c])
            current = ext[it, 3 + c, HALO : HALO + BLOCK, :] * jnp.exp(log_total)
            if it < ITERS - 1:
                ext[it + 1, 3 + c, HALO : HALO + BLOCK, :] = current
            else:
                x2[pl.ds(c, 128, stride=4), :] = current.T

    def q_copy(n, kt, source):
        src = x2.at[pl.ds(pl.multiple_of(64 * slab_of(kt), 64), 64)]
        return remote(src, r3.at[source], q_s.at[n], q_r.at[n], at_kk(xh, core, kt))

    @pl.loop(1, 8)
    def _(n):
        q_copy(n, lax.rem(kk + n, 8), kk).start()

    r3[kk] = x2[mine, :]

    @pl.loop(1, 8)
    def _(n):
        q_copy(n, lax.rem(kk + n, 8), lax.rem(kk + 8 - n, 8)).wait_recv()

    @pl.loop(0, 8)
    def _(m):
        part = pl.ds(pl.multiple_of(8 * m, 8), 8)
        for i in range(4):
            first, second = exchange_halves(r3[2 * i, part, :], r3[2 * i + 1, part, :])
            s4[2 * m, i] = first
            s4[2 * m + 1, i] = second

    def y_copy(d, source, device):
        return remote(s4.at[lax.rem(z + d, NZ)], gathered.at[view, source], y_s.at[d], y_r.at[d], device)

    @pl.loop(0, NZ - 1)
    def _(i):
        d = far_first(i)
        y_copy(d, z, at_z(lax.rem(z + d, NZ))).start()

    gathered[view, z] = s4[z]

    @pl.loop(0, NZ - 1)
    def _(i):
        d = far_first(i)
        y_copy(d, lax.rem(z + NZ - d, NZ), at_z(lax.rem(z + d, NZ))).wait_recv()

    def v_copy(m, source, device):
        return remote(gathered.at[source], gathered.at[source], v_s.at[m], v_r.at[m], device)

    for m in range(1, VIEWS):
        v_copy(m, view, at_view(lax.rem(view + m, VIEWS))).start()
    for m in range(1, VIEWS):
        v_copy(m, lax.rem(view + VIEWS - m, VIEWS), at_view(lax.rem(view + m, VIEWS))).wait_recv()

    @pl.loop(0, NZ)
    def _(zt):
        for h in range(2):
            for i in range(4):
                first, second = exchange_halves(gathered[2 * h, zt, i], gathered[2 * h + 1, zt, i])
                turned[64 * h + 16 * i : 64 * h + 16 * i + 8, :] = first
                turned[64 * h + 16 * i + 8 : 64 * h + 16 * i + 16, :] = second
        out[pl.ds(pl.multiple_of(BLOCK * zt, BLOCK), BLOCK), :] = turned[...].T

    for m in range(1, VIEWS):
        par_copy(m, view, at_view(lax.rem(view + m, VIEWS))).wait_send()
        v_copy(m, view, at_view(lax.rem(view + m, VIEWS))).wait_send()

    @pl.loop(1, NZ)
    def _(d):
        z_copy(d, z, at_z(lax.rem(z + d, NZ))).wait_send()
        y_copy(d, z, at_z(lax.rem(z + d, NZ))).wait_send()

    @pl.loop(1, 32)
    def _(n):
        to = lax.rem(place + n, 32)
        obs_copy(n, g_of(to), view, slab, at_place(to)).wait_send()

    @pl.loop(1, 8)
    def _(n):
        p_copy(n, lax.rem(kk + n, 8), kk).wait_send()
        q_copy(n, lax.rem(kk + n, 8), kk).wait_send()

    for it in range(ITERS):
        for copy in (*ext_columns(it), *ext_rows(it)):
            copy.wait_send()

        @pl.loop(0, VIEWS)
        def _(v):
            for copy in (*spread_columns(it, v), *tall_rows(it, v)):
                copy.wait_send()


def on_device(estimate, observed, long_taps, short_taps, brick_map, valid_rows):
    dma = pltpu.SemaphoreType.DMA
    vmem = pl.BlockSpec(memory_space=pltpu.VMEM)
    scratch = [
        ((VIEWS, 8, 128), F32),
        ((128, 128), F32),
        ((NZ, 4, 8, 128), F32),
        ((NZ, 4, 8, 128), F32),
        ((512, 128), F32),
        ((512, 128), F32),
        ((2048, 128), F32),
        ((VIEWS, 8, 64, 128), F32),
        ((ITERS, WIDE, TALL, 128), F32),
        ((WIDE, VIEWS * BLOCK, 128), F32),
        ((ITERS, VIEWS, WIDE, BLOCK, 128), F32),
        ((ITERS, VIEWS, OWN, TALL, 128), F32),
        ((VIEWS, OWN, BLOCK, 128), F32),
        ((512, 128), F32),
        ((8, 64, 128), F32),
        ((NZ, 4, 8, 128), F32),
        ((VIEWS, NZ, 4, 8, 128), F32),
        ((VIEWS * 8, 128), F32),
        *[((VIEWS, 128, 128), BF16)] * 4,
        *[((VIEWS * BLOCK, TALL), BF16)] * 4,
    ]
    semaphores = [
        (VIEWS,), (VIEWS,), (NZ,), (NZ,), (32,), (32,), (8,), (8,),
        (ITERS, 2), (ITERS, 2), (ITERS, 2), (ITERS, 2),
        (ITERS, VIEWS, 2), (ITERS, VIEWS, 2), (ITERS, VIEWS, 2), (ITERS, VIEWS, 2),
        (8,), (8,), (NZ,), (NZ,), (VIEWS,), (VIEWS,),
    ]
    refined = pl.pallas_call(
        kernel,
        out_shape=jax.ShapeDtypeStruct((ROWS, COLS), F32),
        in_specs=[vmem] * 6,
        out_specs=vmem,
        scratch_shapes=[pltpu.VMEM(s, t) for s, t in scratch] + [dma(s) for s in semaphores],
        compiler_params=pltpu.CompilerParams(
            collective_id=0, has_side_effects=True, vmem_limit_bytes=48 * 2**20
        ),
    )(
        estimate.reshape(ROWS, COLS),
        observed.reshape(BRICKS * 16, COLS),
        long_taps,
        short_taps.reshape(2, 7),
        brick_map,
        valid_rows,
    )
    return refined.reshape(1, ROWS, COLS)


def solution(mesh):
    fine = Mesh(mesh.devices.reshape(2, 2, NZ, NY, 2), AXES)
    view, bricks = ("xh", "core"), ("z", "y", "xl")
    placed = (
        P(bricks, None, None),
        P(view, None, bricks, None),
        P(view, None),
        P(view, None, None),
        P(view, None),
        P(view, None),
    )
    return jax.shard_map(
        on_device, mesh=fine, in_specs=placed, out_specs=P(bricks, None, None), check_vma=False
    )
```

time: 749 us -> 137 us (0.18)
  waiting for transfers between devices: 306 us -> 0 us
  blocking collectives: 198 us -> 0 us
  other arithmetic: 159 us -> 0 us
  Pallas kernels: 0 us -> 133 us
  starting transfers between devices: 46.5 us -> 0 us
  local copies, waits for them, and re-layouts: 23.3 us -> 4.12 us
  between operations: 13.8 us -> 0.03 us
    all_to_all x3 -> x0, blocking collectives: 198 us -> none  [the longest x2 132 us: to_reference(): lax.all_to_all(ordered, 'brick', split_axis=0, concat_axis=1, tiled=True)]
    ppermute x8 -> x0, waiting for transfers between devices: 147 us -> none  [the longest x4 120 us: with_halo(): lax.ppermute(lax.slice_in_dim(block, block.shape[dim] - width, None, axis...]
    add x11 -> x0, other arithmetic: 136 us -> none  [the longest x4 104 us: blur_rows(): summed + kernel[offset] * lax.slice_in_dim(padded, offset, offset + lengt...]
    pallas_call x0 -> x1, Pallas kernels: none -> 133 us  [on_device(): pl.pallas_call(kernel, out_shape=jax.ShapeDtypeStruct((ROWS, COLS), F32),...]
    psum x2 -> x0, waiting for transfers between devices: 116 us -> none  [on_device(): current = current * jnp.exp(lax.psum(log_terms, 'view'))]
    all_to_all x1 -> x0, waiting for transfers between devices: 43.9 us -> none  [to_view(): lax.all_to_all(volume, 'brick', split_axis=1, concat_axis=0, tiled=True)]
    ppermute x8 -> x0, starting transfers between devices: 24.8 us -> none  [the longest x4 19.4 us: with_halo(): lax.ppermute(lax.slice_in_dim(block, block.shape[dim] - width, None, axis...]
    all_to_all x1 -> x0, starting transfers between devices: 21.6 us -> none  [to_view(): lax.all_to_all(volume, 'brick', split_axis=1, concat_axis=0, tiled=True)]
  transfers between devices with their start and end apart: 11 -> 0, of which waited for: 10 -> 0; matrix products, arithmetic and copies ran while one was open for 2% -> 0% of each run, Pallas kernels for 0% -> 0%
where the time goes in v1:
time: 137 us
  Pallas kernels  133 us (97%)
  local copies, waits for them, and re-layouts  4.12 us (3%)
    pallas_call x1, Pallas kernels, on_device(): pl.pallas_call(kernel, out_shape=jax.ShapeDtypeStruct((ROWS, COLS), F32),...  133 us
    unnamed x13, local copies, waits for them, and re-layouts  4.12 us

profile of v1, /device:TPU:1, one launch (start us, length us, event | category | flops | bytes accessed | tf_op | source)
XLA Modules:
  0.0 137.1 jit_solution(7107820633978514190)
XLA Ops:
  0.0 0.0 copy-start.4
  0.0 0.0 copy-start.5
  0.0 0.0 copy-start.2
  0.0 0.0 copy-start.3
  0.0 0.6 copy-done.4
  0.7 0.0 copy-done.5
  0.7 0.0 copy-done.2
  0.7 0.0 copy-done.3
  0.7 0.0 copy-start
  0.7 1.2 copy-done
  1.9 0.0 copy-start.1
  1.9 1.2 copy-done.1
  3.2 133.0 %shard_map.64 = f32[2048,128]{1,0:T(8,128)S(1)} custom-call(f32[2048,128]{1,0:T(8,128)S(1)} %bitcast.5, f32[2048,128]{1,0:T(8,128)S(1)} %bitcast.6, f32[1,31]{1,0:T(1,128)S(1)} %copy-done.3, f32[2,7]{1,0:T(2,128)S(1)} %bitcast.7, s32[1,128]{1,0:T(1,128)S(1)} %copy-done.4, s32[1,128]{1,0:T(1,128)S(1)} %copy-done.5), custom_call_target="tpu_custom_call" | custom-call | tf_op jit(solution)/shard_map/pallas_call | solution.py:444
  136.2 1.0 copy.8
Async XLA Ops:
  0.0 0.7 copy-start.4
  0.0 0.7 copy-start.5
  0.0 0.7 copy-start.2
  0.0 0.7 copy-start.3
  0.7 1.2 copy-start
  1.9 1.2 copy-start.1

commit v2 on v1

--- a/solution.py
+++ b/solution.py
@@ -48,11 +48,11 @@
 
 
 def kernel(
-    est, obs, long_taps, short_taps, brick_map, valid_rows, out,
-    par, turned, s1, r1, s2, r2, obs_out, obs_in, ext, rows_done, spread, tall, corr,
+    est_ref, obs_ref, long_taps, short_taps, brick_map, valid_rows, out,
+    est, obs, par, turned, s1, r1, s2, r2, obs_out, obs_in, ext, rows_done, spread, tall, corr,
     x2, r3, s4, gathered, tile_taps, bf_h, bf_l, bb_h, bb_l, tf_h, tf_l, tb_h, tb_l,
-    par_s, par_r, z_s, z_r, obs_s, obs_r, p_s, p_r, ec_s, ec_r, er_s, er_r, uc_s, uc_r, ur_s, ur_r,
-    q_s, q_r, y_s, y_r, v_s, v_r,
+    par_s, par_r, z_s, z_r, obs_s, obs_r, p_s, p_r, e_s, e_r, uc_s, uc_r, ur_s, ur_r,
+    q_s, q_r, y_s, y_r, core_s, core_r, mate_s, mate_r, next_s, next_r, in_s,
 ):
     xh, core, z, y, xl = (lax.axis_index(a) for a in AXES)
     x = 2 * xh + xl
@@ -71,9 +71,10 @@
         _, _, _, y_, xl_ = at_kk(xh, core, kk_)
         return 2 * y_ + xl_
 
-    def at_g(g_):
+    def at_g(g_, z_=None):
         k_ = g_ // 2
-        return at_kk(k_ // 8, lax.rem(g_, 2), lax.rem(k_, 8))
+        xh_, core_, _, y_, xl_ = at_kk(k_ // 8, lax.rem(g_, 2), lax.rem(k_, 8))
+        return xh_, core_, z if z_ is None else z_, y_, xl_
 
     def at_z(z_):
         return xh, core, z_, y, xl
@@ -94,8 +95,24 @@
             src_ref=src, dst_ref=dst, send_sem=send, recv_sem=recv, device_id=device, device_id_type=MESH
         )
 
+    leaving = []
+
+    def later(first, last, copy):
+        def wait():
+            @pl.loop(first, last)
+            def _(i):
+                copy(i).wait_send()
+
+        leaving.append(wait)
+
     left, right = lax.rem(g + 31, 32), lax.rem(g + 1, 32)
     above, below = lax.rem(z + NZ - 1, NZ), lax.rem(z + 1, NZ)
+
+    loads = [
+        pltpu.make_async_copy(a, b, in_s.at[i]) for i, (a, b) in enumerate(((est_ref, est), (obs_ref, obs)))
+    ]
+    for load in loads:
+        load.start()
 
     barrier = pltpu.get_barrier_semaphore()
 
@@ -106,6 +123,10 @@
     @pl.loop(1, 32)
     def _(n):
         pl.semaphore_signal(barrier, inc=1, device_id=at_place(lax.rem(place + n, 32)), device_id_type=MESH)
+
+    for g_ in (left, right):
+        for z_ in (above, below):
+            pl.semaphore_signal(barrier, inc=1, device_id=at_g(g_, z_), device_id_type=MESH)
 
     par[view] = jnp.zeros((8, 128), F32)
     par[view, 0:1, :] = brick_map[...].astype(F32)
@@ -113,13 +134,16 @@
     par[view, 2:3, 0:31] = long_taps[...]
     par[view, 3:5, 0:7] = short_taps[...]
 
-    pl.semaphore_wait(barrier, NZ - 1 + 31)
+    pl.semaphore_wait(barrier, NZ - 1 + 31 + 4)
 
     def par_copy(m, source, device):
         return remote(par.at[source], par.at[source], par_s.at[m], par_r.at[m], device)
 
     for m in range(1, VIEWS):
         par_copy(m, view, at_view(lax.rem(view + m, VIEWS))).start()
+    later(1, VIEWS, lambda m: par_copy(m, view, at_view(lax.rem(view + m, VIEWS))))
+
+    loads[0].wait()
 
     def piece_for(zt):
         block = est[pl.ds(pl.multiple_of(BLOCK * zt, BLOCK), BLOCK), :]
@@ -141,7 +165,10 @@
         s1[d] = piece_for(zt)
         z_copy(d, z, at_z(zt)).start()
 
+    later(1, NZ, lambda d: z_copy(d, z, at_z(lax.rem(z + d, NZ))))
     r1[z] = piece_for(z)
+
+    loads[1].wait()
 
     @pl.loop(0, 16)
     def _(r):
@@ -156,6 +183,11 @@
         to = lax.rem(place + n, 32)
         obs_copy(n, g_of(to), view, slab, at_place(to)).start()
 
+    def obs_sent(n):
+        to = lax.rem(place + n, 32)
+        return obs_copy(n, g_of(to), view, slab, at_place(to))
+
+    later(1, 32, obs_sent)
     obs_in[view, slab] = obs_out[pl.ds(pl.multiple_of(64 * g, 64), 64), :]
 
     for m in range(1, VIEWS):
@@ -211,6 +243,7 @@
     def _(n):
         p_copy(n, lax.rem(kk + n, 8), kk).start()
 
+    later(1, 8, lambda n: p_copy(n, lax.rem(kk + n, 8), kk))
     mine = pl.ds(pl.multiple_of(64 * slab, 64), 64)
     r2[mine, :] = s2[pl.ds(pl.multiple_of(64 * kk, 64), 64), :]
 
@@ -221,25 +254,38 @@
     for c in range(OWN):
         ext[0, 3 + c, HALO : HALO + BLOCK, :] = r2[pl.ds(c, 128, stride=4), :].T
 
-    @pl.loop(1, 32)
-    def _(n):
-        source = lax.rem(place + 32 - n, 32)
-        to = lax.rem(place + n, 32)
-        obs_copy(n, g_of(to), source // 8, lax.rem(source, 8), at_place(to)).wait_recv()
+    def observed_arrives():
+        @pl.loop(1, 32)
+        def _(n):
+            source = lax.rem(place + 32 - n, 32)
+            to = lax.rem(place + n, 32)
+            obs_copy(n, g_of(to), source // 8, lax.rem(source, 8), at_place(to)).wait_recv()
 
     middle = pl.ds(HALO, BLOCK)
 
-    def ext_columns(it):
+    first, last = pl.ds(HALO, HALO), pl.ds(BLOCK, HALO)
+    before, after = pl.ds(0, HALO), pl.ds(HALO + BLOCK, HALO)
+
+    def ext_copy(it, i, columns, rows, to_columns, to_rows, device):
+        return remote(
+            ext.at[it, columns, rows], ext.at[it, to_columns, to_rows], e_s.at[it, i], e_r.at[it, i], device
+        )
+
+    def ext_sides(it):
         return (
-            remote(ext.at[it, 3:6, middle], ext.at[it, 7:10, middle], ec_s.at[it, 0], ec_r.at[it, 0], at_g(left)),
-            remote(ext.at[it, 4:7, middle], ext.at[it, 0:3, middle], ec_s.at[it, 1], ec_r.at[it, 1], at_g(right)),
+            ext_copy(it, 0, pl.ds(3, 3), middle, pl.ds(7, 3), middle, at_g(left)),
+            ext_copy(it, 1, pl.ds(4, 3), middle, pl.ds(0, 3), middle, at_g(right)),
+            ext_copy(it, 2, pl.ds(3, 3), first, pl.ds(7, 3), after, at_g(left, above)),
+            ext_copy(it, 3, pl.ds(3, 3), last, pl.ds(7, 3), before, at_g(left, below)),
+            ext_copy(it, 4, pl.ds(4, 3), first, pl.ds(0, 3), after, at_g(right, above)),
+            ext_copy(it, 5, pl.ds(4, 3), last, pl.ds(0, 3), before, at_g(right, below)),
         )
 
     def ext_rows(it):
-        first, last = pl.ds(HALO, HALO), pl.ds(BLOCK, HALO)
+        own = pl.ds(3, OWN)
         return (
-            remote(ext.at[it, :, first], ext.at[it, :, pl.ds(HALO + BLOCK, HALO)], er_s.at[it, 0], er_r.at[it, 0], at_z(above)),
-            remote(ext.at[it, :, last], ext.at[it, :, pl.ds(0, HALO)], er_s.at[it, 1], er_r.at[it, 1], at_z(below)),
+            ext_copy(it, 6, own, first, own, after, at_z(above)),
+            ext_copy(it, 7, own, last, own, before, at_z(below)),
         )
 
     def spread_columns(it, v):
@@ -249,10 +295,9 @@
         )
 
     def tall_rows(it, v):
-        first, last = pl.ds(HALO, HALO), pl.ds(BLOCK, HALO)
         return (
-            remote(tall.at[it, v, :, first], tall.at[it, v, :, pl.ds(HALO + BLOCK, HALO)], ur_s.at[it, v, 0], ur_r.at[it, v, 0], at_z(above)),
-            remote(tall.at[it, v, :, last], tall.at[it, v, :, pl.ds(0, HALO)], ur_s.at[it, v, 1], ur_r.at[it, v, 1], at_z(below)),
+            remote(tall.at[it, v, :, first], tall.at[it, v, :, after], ur_s.at[it, v, 0], ur_r.at[it, v, 0], at_z(above)),
+            remote(tall.at[it, v, :, last], tall.at[it, v, :, before], ur_s.at[it, v, 1], ur_r.at[it, v, 1], at_z(below)),
         )
 
     def column_inside(i):
@@ -261,63 +306,113 @@
 
     row_ids = (BLOCK * z + lax.broadcasted_iota(jnp.int32, (BLOCK, 128), 0)).astype(F32)
 
+    def send(copies):
+        for copy in copies:
+            copy.start()
+
+    def arrive(copies):
+        for copy in copies:
+            copy.wait_recv()
+
+    def blur_rows(it, i):
+        head, tail = split(jnp.where(column_inside(i), ext[it, i], 0.0))
+        rows_done[i] = dot3(tf_h[...], tf_l[...], head, tail)
+
+    def back_projected(v, c):
+        part = pl.ds(pl.multiple_of(BLOCK * v, BLOCK), BLOCK)
+        blurred = jnp.zeros((BLOCK, 128), F32)
+        for t in range(7):
+            blurred += tile_taps[pl.ds(8 * v + t, 1), :] * rows_done[c + t, part, :]
+        blurred = dot3(*split(blurred), bf_h[v], bf_l[v])
+        seen = obs_in[v, :, pl.ds(pl.multiple_of(16 * c, 16), 16), :].reshape(BLOCK, 128)
+        ratio = jnp.where(row_ids < par[v, 1:2, :], seen / blurred, 1.0)
+        return dot3(*split(ratio), bb_h[v], bb_l[v])
+
+    def columns_back(it, v, c):
+        total = jnp.zeros((BLOCK, 128), F32)
+        for t in range(7):
+            tap = jnp.where(column_inside(c + t), tile_taps[pl.ds(8 * v + 6 - t, 1), :], 0.0)
+            total += tap * spread[it, v, c + t]
+        return total
+
+    def rows_back(it, v, c):
+        part = pl.ds(pl.multiple_of(BLOCK * v, BLOCK), BLOCK)
+        return dot3(tb_h[part, :], tb_l[part, :], *split(tall[it, v, c]))
+
     for it in range(ITERS):
-        for copy in ext_columns(it):
-            copy.start()
-        for copy in ext_columns(it):
-            copy.wait_recv()
-        for copy in ext_rows(it):
-            copy.start()
-        for copy in ext_rows(it):
-            copy.wait_recv()
-
-        @pl.loop(0, WIDE)
+        send(ext_sides(it))
+        send(ext_rows(it))
+        leaving.extend(copy.wait_send for copy in (*ext_sides(it), *ext_rows(it)))
+        arrive(ext_rows(it))
+
+        @pl.loop(3, 3 + OWN)
         def _(i):
-            head, tail = split(jnp.where(column_inside(i), ext[it, i], 0.0))
-            rows_done[i] = dot3(tf_h[...], tf_l[...], head, tail)
-
-        @pl.loop(0, VIEWS)
+            blur_rows(it, i)
+
+        arrive(ext_sides(it))
+
+        @pl.loop(0, 6)
+        def _(i):
+            blur_rows(it, i + OWN * (i // 3))
+
+        if it == 0:
+            observed_arrives()
+
+        @pl.loop(0, 2)
         def _(v):
-            part = pl.ds(pl.multiple_of(BLOCK * v, BLOCK), BLOCK)
-
             @pl.loop(0, OWN)
             def _(c):
-                blurred = jnp.zeros((BLOCK, 128), F32)
-                for t in range(7):
-                    blurred += tile_taps[pl.ds(8 * v + t, 1), :] * rows_done[c + t, part, :]
-                blurred = dot3(*split(blurred), bf_h[v], bf_l[v])
-                seen = obs_in[v, :, pl.ds(pl.multiple_of(16 * c, 16), 16), :].reshape(BLOCK, 128)
-                ratio = jnp.where(row_ids < par[v, 1:2, :], seen / blurred, 1.0)
-                spread[it, v, 3 + c] = dot3(*split(ratio), bb_h[v], bb_l[v])
-
-            for copy in spread_columns(it, v):
-                copy.start()
-
-        @pl.loop(0, VIEWS)
+                spread[it, v, 3 + c] = back_projected(v, c)
+
+            send(spread_columns(it, v))
+
+        @pl.loop(2, VIEWS)
         def _(v):
-            for copy in spread_columns(it, v):
-                copy.wait_recv()
-
             @pl.loop(0, OWN)
             def _(c):
-                total = jnp.zeros((BLOCK, 128), F32)
-                for t in range(7):
-                    tap = jnp.where(column_inside(c + t), tile_taps[pl.ds(8 * v + 6 - t, 1), :], 0.0)
-                    total += tap * spread[it, v, c + t]
-                tall[it, v, c, HALO : HALO + BLOCK, :] = total
-
-            for copy in tall_rows(it, v):
-                copy.start()
-
-        @pl.loop(0, VIEWS)
+                tall[it, v, c, HALO : HALO + BLOCK, :] = back_projected(v, c)
+
+            send(tall_rows(it, v))
+
+        @pl.loop(2, VIEWS)
         def _(v):
-            for copy in tall_rows(it, v):
-                copy.wait_recv()
-            part = pl.ds(pl.multiple_of(BLOCK * v, BLOCK), BLOCK)
+            arrive(tall_rows(it, v))
 
             @pl.loop(0, OWN)
             def _(c):
-                corr[v, c] = dot3(tb_h[part, :], tb_l[part, :], *split(tall[it, v, c]))
+                spread[it, v, 3 + c] = rows_back(it, v, c)
+
+            send(spread_columns(it, v))
+
+        @pl.loop(0, 2)
+        def _(v):
+            arrive(spread_columns(it, v))
+
+            @pl.loop(0, OWN)
+            def _(c):
+                tall[it, v, c, HALO : HALO + BLOCK, :] = columns_back(it, v, c)
+
+            send(tall_rows(it, v))
+
+        @pl.loop(0, 2)
+        def _(v):
+            arrive(tall_rows(it, v))
+
+            @pl.loop(0, OWN)
+            def _(c):
+                corr[v, c] = rows_back(it, v, c)
+
+        @pl.loop(2, VIEWS)
+        def _(v):
+            arrive(spread_columns(it, v))
+
+            @pl.loop(0, OWN)
+            def _(c):
+                corr[v, c] = columns_back(it, v, c)
+
+        for i in range(2):
+            later(0, VIEWS, lambda v, i=i, it=it: spread_columns(it, v)[i])
+            later(0, VIEWS, lambda v, i=i, it=it: tall_rows(it, v)[i])
 
         for c in range(OWN):
             log_total = jnp.log(corr[0, c] * corr[1, c]) + jnp.log(corr[2, c] * corr[3, c])
@@ -335,6 +430,7 @@
     def _(n):
         q_copy(n, lax.rem(kk + n, 8), kk).start()
 
+    later(1, 8, lambda n: q_copy(n, lax.rem(kk + n, 8), kk))
     r3[kk] = x2[mine, :]
 
     @pl.loop(1, 8)
@@ -349,71 +445,86 @@
             s4[2 * m, i] = first
             s4[2 * m + 1, i] = second
 
-    def y_copy(d, source, device):
-        return remote(s4.at[lax.rem(z + d, NZ)], gathered.at[view, source], y_s.at[d], y_r.at[d], device)
-
-    @pl.loop(0, NZ - 1)
+    def y_copy(i, device):
+        d = far_first(i - 1)
+        return remote(s4.at[lax.rem(z + d, NZ)], gathered.at[view, i], y_s.at[i], y_r.at[i], device)
+
+    def y_sent(i):
+        return y_copy(i, at_z(lax.rem(z + far_first(i - 1), NZ)))
+
+    @pl.loop(1, NZ)
     def _(i):
-        d = far_first(i)
-        y_copy(d, z, at_z(lax.rem(z + d, NZ))).start()
-
-    gathered[view, z] = s4[z]
-
-    @pl.loop(0, NZ - 1)
-    def _(i):
-        d = far_first(i)
-        y_copy(d, lax.rem(z + NZ - d, NZ), at_z(lax.rem(z + d, NZ))).wait_recv()
-
-    def v_copy(m, source, device):
-        return remote(gathered.at[source], gathered.at[source], v_s.at[m], v_r.at[m], device)
-
-    for m in range(1, VIEWS):
-        v_copy(m, view, at_view(lax.rem(view + m, VIEWS))).start()
-    for m in range(1, VIEWS):
-        v_copy(m, lax.rem(view + VIEWS - m, VIEWS), at_view(lax.rem(view + m, VIEWS))).wait_recv()
-
-    @pl.loop(0, NZ)
-    def _(zt):
-        for h in range(2):
-            for i in range(4):
-                first, second = exchange_halves(gathered[2 * h, zt, i], gathered[2 * h + 1, zt, i])
-                turned[64 * h + 16 * i : 64 * h + 16 * i + 8, :] = first
-                turned[64 * h + 16 * i + 8 : 64 * h + 16 * i + 16, :] = second
-        out[pl.ds(pl.multiple_of(BLOCK * zt, BLOCK), BLOCK), :] = turned[...].T
-
-    for m in range(1, VIEWS):
-        par_copy(m, view, at_view(lax.rem(view + m, VIEWS))).wait_send()
-        v_copy(m, view, at_view(lax.rem(view + m, VIEWS))).wait_send()
-
-    @pl.loop(1, NZ)
-    def _(d):
-        z_copy(d, z, at_z(lax.rem(z + d, NZ))).wait_send()
-        y_copy(d, z, at_z(lax.rem(z + d, NZ))).wait_send()
-
-    @pl.loop(1, 32)
-    def _(n):
-        to = lax.rem(place + n, 32)
-        obs_copy(n, g_of(to), view, slab, at_place(to)).wait_send()
-
-    @pl.loop(1, 8)
-    def _(n):
-        p_copy(n, lax.rem(kk + n, 8), kk).wait_send()
-        q_copy(n, lax.rem(kk + n, 8), kk).wait_send()
-
-    for it in range(ITERS):
-        for copy in (*ext_columns(it), *ext_rows(it)):
-            copy.wait_send()
-
-        @pl.loop(0, VIEWS)
-        def _(v):
-            for copy in (*spread_columns(it, v), *tall_rows(it, v)):
-                copy.wait_send()
+        y_sent(i).start()
+
+    later(1, NZ, y_sent)
+    gathered[view, 0] = s4[z]
+
+    other_core, other_chip = (xh, 1 - core, z, y, xl), (1 - xh, core, z, y, xl)
+    over = 2 * (1 - xh) + core
+
+    def pass_on(j, owner, send_sem, recv_sem, device):
+        blocks = gathered.at[owner, pl.ds(pl.multiple_of(4 * j, 4), 4)]
+        return remote(blocks, blocks, send_sem.at[j], recv_sem.at[j], device)
+
+    def to_core(j):
+        return pass_on(j, view, core_s, core_r, other_core)
+
+    def to_chip(j):
+        return pass_on(j, view, mate_s, mate_r, other_chip)
+
+    def onward(j):
+        return pass_on(j, over, next_s, next_r, other_core)
+
+    for copy in (to_core, to_chip, onward):
+        later(0, NZ // 4, copy)
+
+    def finish(j):
+        pass_on(j, 2 * xh + 1 - core, core_s, core_r, other_core).wait_recv()
+        pass_on(j, 2 * (1 - xh) + 1 - core, next_s, next_r, other_core).wait_recv()
+
+        @pl.loop(0, 4)
+        def _(n):
+            i = 4 * j + n
+            zt = lax.rem(z + NZ - jnp.where(i == 0, 0, far_first(i - 1)), NZ)
+            for h in range(2):
+                for t in range(4):
+                    a, b = exchange_halves(gathered[2 * h, i, t], gathered[2 * h + 1, i, t])
+                    turned[64 * h + 16 * t : 64 * h + 16 * t + 8, :] = a
+                    turned[64 * h + 16 * t + 8 : 64 * h + 16 * t + 16, :] = b
+            out[pl.ds(pl.multiple_of(BLOCK * zt, BLOCK), BLOCK), :] = turned[...].T
+
+    @pl.loop(0, NZ // 4)
+    def _(j):
+        @pl.loop(jnp.where(j == 0, 1, 4 * j), 4 * j + 4)
+        def _(i):
+            y_sent(i).wait_recv()
+
+        to_chip(j).start()
+        to_core(j).start()
+
+        @pl.when(j > 0)
+        def _():
+            pass_on(j - 1, over, mate_s, mate_r, other_chip).wait_recv()
+            onward(j - 1).start()
+
+    end = NZ // 4 - 1
+    pass_on(end, over, mate_s, mate_r, other_chip).wait_recv()
+    onward(end).start()
+
+    @pl.loop(0, NZ // 4)
+    def _(j):
+        finish(j)
+
+    for wait in leaving:
+        wait()
 
 
 def on_device(estimate, observed, long_taps, short_taps, brick_map, valid_rows):
     dma = pltpu.SemaphoreType.DMA
     vmem = pl.BlockSpec(memory_space=pltpu.VMEM)
     scratch = [
+        ((ROWS, COLS), F32),
+        ((ROWS, COLS), F32),
         ((VIEWS, 8, 128), F32),
         ((128, 128), F32),
         ((NZ, 4, 8, 128), F32),
@@ -437,18 +548,18 @@
     ]
     semaphores = [
         (VIEWS,), (VIEWS,), (NZ,), (NZ,), (32,), (32,), (8,), (8,),
-        (ITERS, 2), (ITERS, 2), (ITERS, 2), (ITERS, 2),
+        (ITERS, 8), (ITERS, 8),
         (ITERS, VIEWS, 2), (ITERS, VIEWS, 2), (ITERS, VIEWS, 2), (ITERS, VIEWS, 2),
-        (8,), (8,), (NZ,), (NZ,), (VIEWS,), (VIEWS,),
+        (8,), (8,), (NZ,), (NZ,), (4,), (4,), (4,), (4,), (4,), (4,), (2,),
     ]
     refined = pl.pallas_call(
         kernel,
         out_shape=jax.ShapeDtypeStruct((ROWS, COLS), F32),
-        in_specs=[vmem] * 6,
+        in_specs=[pl.BlockSpec(memory_space=pl.ANY)] * 2 + [vmem] * 4,
         out_specs=vmem,
         scratch_shapes=[pltpu.VMEM(s, t) for s, t in scratch] + [dma(s) for s in semaphores],
         compiler_params=pltpu.CompilerParams(
-            collective_id=0, has_side_effects=True, vmem_limit_bytes=48 * 2**20
+            collective_id=0, has_side_effects=True, vmem_limit_bytes=56 * 2**20
         ),
     )(
         estimate.reshape(ROWS, COLS),

time: 137 us -> 120 us (0.88)
  Pallas kernels: 133 us -> 118 us
  local copies, waits for them, and re-layouts: 4.12 us -> 2.26 us
    pallas_call x1, Pallas kernels: 133 us -> 118 us  [on_device(): pl.pallas_call(kernel, out_shape=jax.ShapeDtypeStruct((ROWS, COLS), F32),...]
    unnamed x13 -> x1, local copies, waits for them, and re-layouts: 4.12 us -> 2.26 us
where the time goes in v2:
time: 120 us
  Pallas kernels  118 us (98%)
  local copies, waits for them, and re-layouts  2.26 us (2%)
    pallas_call x1, Pallas kernels, on_device(): pl.pallas_call(kernel, out_shape=jax.ShapeDtypeStruct((ROWS, COLS), F32),...  118 us

profile of v2, /device:TPU:1, one launch (start us, length us, event | category | flops | bytes accessed | tf_op | source)
XLA Modules:
  0.0 120.0 jit_solution(8900776630655129271)
XLA Ops:
  0.0 117.7 %shard_map.64 = f32[2048,128]{1,0:T(8,128)} custom-call(f32[2048,128]{1,0:T(8,128)} %bitcast.5, f32[2048,128]{1,0:T(8,128)} %bitcast.6, f32[1,31]{1,0:T(1,128)} %long_taps.1, f32[2,7]{1,0:T(2,128)} %bitcast.7, s32[1,128]{1,0:T(1,128)} %brick_map.1, s32[1,128]{1,0:T(1,128)} %valid_rows.1), custom_call_target="tpu_custom_call" | custom-call | tf_op jit(solution)/shard_map/pallas_call | solution.py:555
  117.7 2.3 %copy.8 = f32[1,2048,128]{2,1,0:T(8,128)} copy(f32[1,2048,128]{2,1,0:T(8,128)} %bitcast.4) | data formatting | bytes 2097152

commit v3 on v2

--- a/solution.py
+++ b/solution.py
@@ -31,6 +31,18 @@
     return dot(ah, bh) + (dot(al, bh) + dot(ah, bl))
 
 
+def doubled(matrix):
+    head, tail = split(matrix)
+    return jnp.concatenate(
+        [jnp.concatenate([head, tail], axis=1), jnp.concatenate([head, jnp.zeros_like(tail)], axis=1)], axis=0
+    )
+
+
+def product(x, twice):
+    both = jnp.dot(jnp.concatenate(split(x), axis=1), twice, preferred_element_type=F32)
+    return both[:, :128] + both[:, 128:]
+
+
 def exchange_halves(a, b):
     axis = a.ndim - 2
     top = lax.broadcasted_iota(jnp.int32, a.shape, axis) < 4
@@ -50,7 +62,7 @@
 def kernel(
     est_ref, obs_ref, long_taps, short_taps, brick_map, valid_rows, out,
     est, obs, par, turned, s1, r1, s2, r2, obs_out, obs_in, ext, rows_done, spread, tall, corr,
-    x2, r3, s4, gathered, tile_taps, bf_h, bf_l, bb_h, bb_l, tf_h, tf_l, tb_h, tb_l,
+    x2, r3, s4, gathered, tile_taps, ahead, back, tf_h, tf_l, tb_h, tb_l,
     par_s, par_r, z_s, z_r, obs_s, obs_r, p_s, p_r, e_s, e_r, uc_s, uc_r, ur_s, ur_r,
     q_s, q_r, y_s, y_r, core_s, core_r, mate_s, mate_r, next_s, next_r, in_s,
 ):
@@ -208,8 +220,7 @@
             near = jnp.where(jnp.logical_and(lane + (t - 3) >= 0, lane + (t - 3) < BRICKS), near, -1.0)
             matrix += jnp.where(brick == near, plane[:, t : t + 1], 0.0)
             tile_taps[8 * v + t : 8 * v + t + 1, :] = jnp.broadcast_to(column[:, t : t + 1], (1, 128))
-        bf_h[v], bf_l[v] = split(matrix)
-        bb_h[v], bb_l[v] = split(matrix.T)
+        ahead[v], back[v] = doubled(matrix), doubled(matrix.T)
         padded = jnp.concatenate([long_row, jnp.zeros((1, 128), F32)], axis=1)
         wide = jnp.broadcast_to(padded, (BLOCK, 256))
         toeplitz = pltpu.roll(wide, 1, 1, stride=1, stride_axis=0)[:, :TALL]
@@ -314,19 +325,24 @@
         for copy in copies:
             copy.wait_recv()
 
-    def blur_rows(it, i):
-        head, tail = split(jnp.where(column_inside(i), ext[it, i], 0.0))
-        rows_done[i] = dot3(tf_h[...], tf_l[...], head, tail)
-
-    def back_projected(v, c):
+    def blur_rows(it, i, j):
+        pair = jnp.concatenate([jnp.where(column_inside(n), ext[it, n], 0.0) for n in (i, j)], axis=1)
+        done = dot3(tf_h[...], tf_l[...], *split(pair))
+        rows_done[i], rows_done[j] = done[:, :128], done[:, 128:]
+
+    def back_projected(v):
         part = pl.ds(pl.multiple_of(BLOCK * v, BLOCK), BLOCK)
-        blurred = jnp.zeros((BLOCK, 128), F32)
-        for t in range(7):
-            blurred += tile_taps[pl.ds(8 * v + t, 1), :] * rows_done[c + t, part, :]
-        blurred = dot3(*split(blurred), bf_h[v], bf_l[v])
-        seen = obs_in[v, :, pl.ds(pl.multiple_of(16 * c, 16), 16), :].reshape(BLOCK, 128)
-        ratio = jnp.where(row_ids < par[v, 1:2, :], seen / blurred, 1.0)
-        return dot3(*split(ratio), bb_h[v], bb_l[v])
+        taps = [tile_taps[pl.ds(8 * v + t, 1), :] for t in range(7)]
+        blurred = jnp.concatenate(
+            [sum(taps[t] * rows_done[c + t, part, :] for t in range(7)) for c in range(OWN)], axis=0
+        )
+        blurred = product(blurred, ahead[v])
+        ratios = []
+        for c in range(OWN):
+            seen = obs_in[v, :, 16 * c : 16 * c + 16, :].reshape(BLOCK, 128)
+            ratio = seen / blurred[BLOCK * c : BLOCK * c + BLOCK]
+            ratios.append(jnp.where(row_ids < par[v, 1:2, :], ratio, 1.0))
+        return product(jnp.concatenate(ratios, axis=0), back[v]).reshape(OWN, BLOCK, 128)
 
     def columns_back(it, v, c):
         total = jnp.zeros((BLOCK, 128), F32)
@@ -335,9 +351,11 @@
             total += tap * spread[it, v, c + t]
         return total
 
-    def rows_back(it, v, c):
+    def rows_back(it, v):
         part = pl.ds(pl.multiple_of(BLOCK * v, BLOCK), BLOCK)
-        return dot3(tb_h[part, :], tb_l[part, :], *split(tall[it, v, c]))
+        beside = jnp.concatenate([tall[it, v, c] for c in range(OWN)], axis=1)
+        done = dot3(tb_h[part, :], tb_l[part, :], *split(beside))
+        return [done[:, 128 * c : 128 * c + 128] for c in range(OWN)]
 
     for it in range(ITERS):
         send(ext_sides(it))
@@ -345,43 +363,35 @@
         leaving.extend(copy.wait_send for copy in (*ext_sides(it), *ext_rows(it)))
         arrive(ext_rows(it))
 
-        @pl.loop(3, 3 + OWN)
+        @pl.loop(0, 2)
         def _(i):
-            blur_rows(it, i)
+            blur_rows(it, 3 + 2 * i, 4 + 2 * i)
 
         arrive(ext_sides(it))
 
-        @pl.loop(0, 6)
+        @pl.loop(0, 3)
         def _(i):
-            blur_rows(it, i + OWN * (i // 3))
+            blur_rows(it, 2 * i + 4 * (i // 2), 1 + 6 * ((i + 1) // 2) + 2 * (i // 2))
 
         if it == 0:
             observed_arrives()
 
         @pl.loop(0, 2)
         def _(v):
-            @pl.loop(0, OWN)
-            def _(c):
-                spread[it, v, 3 + c] = back_projected(v, c)
-
+            spread[it, v, 3 : 3 + OWN] = back_projected(v)
             send(spread_columns(it, v))
 
         @pl.loop(2, VIEWS)
         def _(v):
-            @pl.loop(0, OWN)
-            def _(c):
-                tall[it, v, c, HALO : HALO + BLOCK, :] = back_projected(v, c)
-
+            tall[it, v, :, HALO : HALO + BLOCK, :] = back_projected(v)
             send(tall_rows(it, v))
 
         @pl.loop(2, VIEWS)
         def _(v):
             arrive(tall_rows(it, v))
 
-            @pl.loop(0, OWN)
-            def _(c):
-                spread[it, v, 3 + c] = rows_back(it, v, c)
-
+            for c, done in enumerate(rows_back(it, v)):
+                spread[it, v, 3 + c] = done
             send(spread_columns(it, v))
 
         @pl.loop(0, 2)
@@ -398,9 +408,8 @@
         def _(v):
             arrive(tall_rows(it, v))
 
-            @pl.loop(0, OWN)
-            def _(c):
-                corr[v, c] = rows_back(it, v, c)
+            for c, done in enumerate(rows_back(it, v)):
+                corr[v, c] = done
 
         @pl.loop(2, VIEWS)
         def _(v):
@@ -543,7 +552,7 @@
         ((NZ, 4, 8, 128), F32),
         ((VIEWS, NZ, 4, 8, 128), F32),
         ((VIEWS * 8, 128), F32),
-        *[((VIEWS, 128, 128), BF16)] * 4,
+        *[((VIEWS, 256, 256), BF16)] * 2,
         *[((VIEWS * BLOCK, TALL), BF16)] * 4,
     ]
     semaphores = [

time: 120 us -> 109 us (0.908)
  Pallas kernels: 118 us -> 106 us
    pallas_call x1, Pallas kernels: 118 us -> 106 us  [on_device(): pl.pallas_call(kernel, out_shape=jax.ShapeDtypeStruct((ROWS, COLS), F32),...]
where the time goes in v3:
time: 109 us
  Pallas kernels  106 us (97%)
  local copies, waits for them, and re-layouts  2.26 us (2%)
    pallas_call x1, Pallas kernels, on_device(): pl.pallas_call(kernel, out_shape=jax.ShapeDtypeStruct((ROWS, COLS), F32),...  106 us
    unnamed x1, local copies, waits for them, and re-layouts  2.26 us

profile of v3, /device:TPU:1, one launch (start us, length us, event | category | flops | bytes accessed | tf_op | source)
XLA Modules:
  0.0 108.7 jit_solution(7530798740064907657)
XLA Ops:
  0.0 106.4 %shard_map.64 = f32[2048,128]{1,0:T(8,128)} custom-call(f32[2048,128]{1,0:T(8,128)} %bitcast.5, f32[2048,128]{1,0:T(8,128)} %bitcast.6, f32[1,31]{1,0:T(1,128)} %long_taps.1, f32[2,7]{1,0:T(2,128)} %bitcast.7, s32[1,128]{1,0:T(1,128)} %brick_map.1, s32[1,128]{1,0:T(1,128)} %valid_rows.1), custom_call_target="tpu_custom_call" | custom-call | tf_op jit(solution)/shard_map/pallas_call | solution.py:564
  106.4 2.3 %copy.8 = f32[1,2048,128]{2,1,0:T(8,128)} copy(f32[1,2048,128]{2,1,0:T(8,128)} %bitcast.4) | data formatting | bytes 2097152

commit v4 on v3

--- a/solution.py
+++ b/solution.py
@@ -60,11 +60,11 @@
 
 
 def kernel(
-    est_ref, obs_ref, long_taps, short_taps, brick_map, valid_rows, out,
-    est, obs, par, turned, s1, r1, s2, r2, obs_out, obs_in, ext, rows_done, spread, tall, corr,
+    est_ref, obs_ref, long_ref, short_ref, map_ref, valid_ref, out,
+    est, obs, long_taps, short_taps, brick_map, valid_rows, res, par, turned, s1, r1, s2, r2, obs_out, obs_in, ext, rows_done, spread, tall, corr,
     x2, r3, s4, gathered, tile_taps, ahead, back, tf_h, tf_l, tb_h, tb_l,
     par_s, par_r, z_s, z_r, obs_s, obs_r, p_s, p_r, e_s, e_r, uc_s, uc_r, ur_s, ur_r,
-    q_s, q_r, y_s, y_r, core_s, core_r, mate_s, mate_r, next_s, next_r, in_s,
+    q_s, q_r, y_s, y_r, core_s, core_r, mate_s, mate_r, next_s, next_r, in_s, out_s,
 ):
     xh, core, z, y, xl = (lax.axis_index(a) for a in AXES)
     x = 2 * xh + xl
@@ -109,19 +109,23 @@
 
     leaving = []
 
-    def later(first, last, copy):
+    def later(first, last, copy, local=False):
         def wait():
             @pl.loop(first, last)
             def _(i):
-                copy(i).wait_send()
+                copy(i).wait() if local else copy(i).wait_send()
 
         leaving.append(wait)
 
     left, right = lax.rem(g + 31, 32), lax.rem(g + 1, 32)
     above, below = lax.rem(z + NZ - 1, NZ), lax.rem(z + 1, NZ)
 
+    pairs = (
+        (est_ref, est), (obs_ref, obs), (long_ref, long_taps), (short_ref, short_taps), (map_ref, brick_map),
+        (valid_ref, valid_rows),
+    )
     loads = [
-        pltpu.make_async_copy(a, b, in_s.at[i]) for i, (a, b) in enumerate(((est_ref, est), (obs_ref, obs)))
+        pltpu.make_async_copy(a, b, in_s.at[i]) for i, (a, b) in enumerate(pairs)
     ]
     for load in loads:
         load.start()
@@ -139,21 +143,15 @@
     for g_ in (left, right):
         for z_ in (above, below):
             pl.semaphore_signal(barrier, inc=1, device_id=at_g(g_, z_), device_id_type=MESH)
+
+    for load in loads[2:]:
+        load.wait()
 
     par[view] = jnp.zeros((8, 128), F32)
     par[view, 0:1, :] = brick_map[...].astype(F32)
     par[view, 1:2, :] = valid_rows[...].astype(F32)
     par[view, 2:3, 0:31] = long_taps[...]
     par[view, 3:5, 0:7] = short_taps[...]
-
-    pl.semaphore_wait(barrier, NZ - 1 + 31 + 4)
-
-    def par_copy(m, source, device):
-        return remote(par.at[source], par.at[source], par_s.at[m], par_r.at[m], device)
-
-    for m in range(1, VIEWS):
-        par_copy(m, view, at_view(lax.rem(view + m, VIEWS))).start()
-    later(1, VIEWS, lambda m: par_copy(m, view, at_view(lax.rem(view + m, VIEWS))))
 
     loads[0].wait()
 
@@ -170,21 +168,33 @@
     def far_first(i):
         return 8 + ((i + 1) // 2) * (1 - 2 * lax.rem(i, 2))
 
+    @pl.loop(1, NZ)
+    def _(d):
+        s1[d] = piece_for(lax.rem(z + d, NZ))
+
+    r1[z] = piece_for(z)
+
+    loads[1].wait()
+
+    @pl.loop(0, 16)
+    def _(r):
+        obs_out[pl.ds(r, 128, stride=16), :] = obs[pl.ds(r, 128, stride=16), :].T
+
+    pl.semaphore_wait(barrier, NZ - 1 + 31 + 4)
+
+    def par_copy(m, source, device):
+        return remote(par.at[source], par.at[source], par_s.at[m], par_r.at[m], device)
+
+    for m in range(1, VIEWS):
+        par_copy(m, view, at_view(lax.rem(view + m, VIEWS))).start()
+    later(1, VIEWS, lambda m: par_copy(m, view, at_view(lax.rem(view + m, VIEWS))))
+
     @pl.loop(0, NZ - 1)
     def _(i):
         d = far_first(i)
-        zt = lax.rem(z + d, NZ)
-        s1[d] = piece_for(zt)
-        z_copy(d, z, at_z(zt)).start()
+        z_copy(d, z, at_z(lax.rem(z + d, NZ))).start()
 
     later(1, NZ, lambda d: z_copy(d, z, at_z(lax.rem(z + d, NZ))))
-    r1[z] = piece_for(z)
-
-    loads[1].wait()
-
-    @pl.loop(0, 16)
-    def _(r):
-        obs_out[pl.ds(r, 128, stride=16), :] = obs[pl.ds(r, 128, stride=16), :].T
 
     def obs_copy(n, g_, view_, slab_, device):
         src = obs_out.at[pl.ds(pl.multiple_of(64 * g_, 64), 64)]
@@ -484,8 +494,21 @@
     def onward(j):
         return pass_on(j, over, next_s, next_r, other_core)
 
-    for copy in (to_core, to_chip, onward):
-        later(0, NZ // 4, copy)
+    def from_chip(j):
+        return pass_on(j, over, mate_s, mate_r, other_chip)
+
+    straight = pass_on(NZ // 4 - 1, view, next_s, next_r, (1 - xh, 1 - core, z, y, xl))
+    later(0, NZ // 4, to_core)
+    later(0, NZ // 4, to_chip)
+    later(0, NZ // 4 - 1, onward)
+    leaving.append(straight.wait_send)
+
+    def block_of(i):
+        return lax.rem(z + NZ - jnp.where(i == 0, 0, far_first(i - 1)), NZ)
+
+    def out_copy(i):
+        rows = pl.ds(pl.multiple_of(BLOCK * block_of(i), BLOCK), BLOCK)
+        return pltpu.make_async_copy(res.at[rows], out.at[rows], out_s.at[i])
 
     def finish(j):
         pass_on(j, 2 * xh + 1 - core, core_s, core_r, other_core).wait_recv()
@@ -494,35 +517,37 @@
         @pl.loop(0, 4)
         def _(n):
             i = 4 * j + n
-            zt = lax.rem(z + NZ - jnp.where(i == 0, 0, far_first(i - 1)), NZ)
+            zt = block_of(i)
             for h in range(2):
                 for t in range(4):
                     a, b = exchange_halves(gathered[2 * h, i, t], gathered[2 * h + 1, i, t])
                     turned[64 * h + 16 * t : 64 * h + 16 * t + 8, :] = a
                     turned[64 * h + 16 * t + 8 : 64 * h + 16 * t + 16, :] = b
-            out[pl.ds(pl.multiple_of(BLOCK * zt, BLOCK), BLOCK), :] = turned[...].T
-
-    @pl.loop(0, NZ // 4)
-    def _(j):
-        @pl.loop(jnp.where(j == 0, 1, 4 * j), 4 * j + 4)
+            rows = pl.ds(pl.multiple_of(BLOCK * zt, BLOCK), BLOCK)
+            res[rows, :] = turned[...].T
+            out_copy(i).start()
+
+    end = NZ // 4 - 1
+    for j in range(NZ // 4):
+
+        @pl.loop(max(1, 4 * j), 4 * j + 4)
         def _(i):
             y_sent(i).wait_recv()
 
         to_chip(j).start()
+        if j == end:
+            straight.start()
         to_core(j).start()
-
-        @pl.when(j > 0)
-        def _():
-            pass_on(j - 1, over, mate_s, mate_r, other_chip).wait_recv()
+        if j > 0:
+            from_chip(j - 1).wait_recv()
             onward(j - 1).start()
-
-    end = NZ // 4 - 1
-    pass_on(end, over, mate_s, mate_r, other_chip).wait_recv()
-    onward(end).start()
-
-    @pl.loop(0, NZ // 4)
-    def _(j):
-        finish(j)
+        if j > 1:
+            finish(j - 2)
+    finish(end - 1)
+    from_chip(end).wait_recv()
+    finish(end)
+
+    later(0, NZ, out_copy, local=True)
 
     for wait in leaving:
         wait()
@@ -530,9 +555,14 @@
 
 def on_device(estimate, observed, long_taps, short_taps, brick_map, valid_rows):
     dma = pltpu.SemaphoreType.DMA
-    vmem = pl.BlockSpec(memory_space=pltpu.VMEM)
+    there = pl.BlockSpec(memory_space=pl.ANY)
     scratch = [
         ((ROWS, COLS), F32),
+        ((ROWS, COLS), F32),
+        ((1, 31), F32),
+        ((2, 7), F32),
+        ((1, 128), jnp.int32),
+        ((1, 128), jnp.int32),
         ((ROWS, COLS), F32),
         ((VIEWS, 8, 128), F32),
         ((128, 128), F32),
@@ -559,13 +589,13 @@
         (VIEWS,), (VIEWS,), (NZ,), (NZ,), (32,), (32,), (8,), (8,),
         (ITERS, 8), (ITERS, 8),
         (ITERS, VIEWS, 2), (ITERS, VIEWS, 2), (ITERS, VIEWS, 2), (ITERS, VIEWS, 2),
-        (8,), (8,), (NZ,), (NZ,), (4,), (4,), (4,), (4,), (4,), (4,), (2,),
+        (8,), (8,), (NZ,), (NZ,), (4,), (4,), (4,), (4,), (4,), (4,), (6,), (NZ,),
     ]
     refined = pl.pallas_call(
         kernel,
         out_shape=jax.ShapeDtypeStruct((ROWS, COLS), F32),
-        in_specs=[pl.BlockSpec(memory_space=pl.ANY)] * 2 + [vmem] * 4,
-        out_specs=vmem,
+        in_specs=[there] * 6,
+        out_specs=there,
         scratch_shapes=[pltpu.VMEM(s, t) for s, t in scratch] + [dma(s) for s in semaphores],
         compiler_params=pltpu.CompilerParams(
             collective_id=0, has_side_effects=True, vmem_limit_bytes=56 * 2**20

time: 109 us -> 106 us (0.972)
  Pallas kernels: 106 us -> 103 us
    pallas_call x1, Pallas kernels: 106 us -> 103 us  [on_device(): pl.pallas_call(kernel, out_shape=jax.ShapeDtypeStruct((ROWS, COLS), F32),...]
where the time goes in v4:
time: 106 us
  Pallas kernels  103 us (97%)
  local copies, waits for them, and re-layouts  2.26 us (2%)
    pallas_call x1, Pallas kernels, on_device(): pl.pallas_call(kernel, out_shape=jax.ShapeDtypeStruct((ROWS, COLS), F32),...  103 us
    unnamed x1, local copies, waits for them, and re-layouts  2.26 us

profile of v4, /device:TPU:1, one launch (start us, length us, event | category | flops | bytes accessed | tf_op | source)
XLA Modules:
  0.0 105.7 jit_solution(8226405038201100040)
XLA Ops:
  0.0 103.4 %shard_map.64 = f32[2048,128]{1,0:T(8,128)} custom-call(f32[2048,128]{1,0:T(8,128)} %bitcast.5, f32[2048,128]{1,0:T(8,128)} %bitcast.6, f32[1,31]{1,0:T(1,128)} %long_ref.1, f32[2,7]{1,0:T(2,128)} %bitcast.7, s32[1,128]{1,0:T(1,128)} %map_ref.1, s32[1,128]{1,0:T(1,128)} %valid_ref.1), custom_call_target="tpu_custom_call" | custom-call | tf_op jit(solution)/shard_map/pallas_call | solution.py:594
  103.4 2.3 %copy.8 = f32[1,2048,128]{2,1,0:T(8,128)} copy(f32[1,2048,128]{2,1,0:T(8,128)} %bitcast.4) | data formatting | bytes 2097152
